TPU v7x, 512 devices: a whole 4x8x8 slice. The times are simulated.
512 devices in a mesh: dp: 128 (over y, z_lo, x), seq: 4 (over z_hi, core).
Axes of the slice: x: 4, y: 8, z: 8 (z_hi: 2, z_lo: 4; z = z_hi * 4 + z_lo), core: 2. Of those that a mesh axis runs over, the one named last changes fastest.
Arguments:
- queries: bfloat16 [128, 512, 4096], P('dp', 'seq'), may hold values from -240 to 240
- encodings: bfloat16 [128, 8, 256, 448], P('dp', 'seq'), may hold values from -6 to 6
- neighbour_ids: int32 [128, 8, 256], P('dp', 'seq'), may hold values from 0 to 31999, as said below
- w_key: bfloat16 [448, 4096], P(None, 'dp'), may hold values from -0.25 to 0.25
- w_value: bfloat16 [448, 4096], P(None, 'dp'), may hold values from -0.25 to 0.25
- cotangent: bfloat16 [128, 512, 4096], P('dp', 'seq'), may hold values from -6 to 6
Outputs:
- attended: bfloat16 [128, 512, 4096], P('dp', 'seq')
- query_grad: bfloat16 [128, 512, 4096], P('dp', 'seq')
Inputs may be any that keep to these rules, and one draw needn't show every extreme that they name: `neighbour_ids`: 0 marks padding: each of the 2 neighbours of a block holds its real token ids (1 or more) first, at least 32 of them, and zeros after them.
All inputs are finite; a program needn't handle non-finite values.
Results may differ from a plain program's by a relative error of at most 0.023.
The roundings to bfloat16 on the way count: a program that leaves them out, or rounds other values in their place, can miss the bound.
Values may be sent and summed in bfloat16 or wider, within the bound.
A program may use at most 128 MiB of HBM per device.

v0:
```python
import jax
import jax.numpy as jnp
from jax import lax
from jax.sharding import PartitionSpec as P

HD = 128
BLOCK = 64


def passed_along(block, axis, distance):
    devices = range(lax.axis_size(axis))
    route = [(i - distance, i) for i in devices if i - distance in devices]
    return lax.ppermute(block, axis, route)


def project(code_rows, stacked):
    return jnp.einsum(
        "re,tec->trc",
        code_rows,
        lax.all_gather(stacked, "dp", axis=2, tiled=True),
        preferred_element_type=jnp.float32,
    ).astype(jnp.bfloat16)


def attend(query_groups, grad_groups, pairs, validity):
    groups = pairs.shape[1]
    key_count = pairs.shape[2]
    heads = query_groups.shape[2]
    key_heads = pairs[0].reshape(groups, key_count, heads, HD)
    value_heads = pairs[1].reshape(groups, key_count, heads, HD)
    factor = HD ** (-0.5)
    scores = (
        jnp.einsum("gqhd,gkhd->ghqk", query_groups, key_heads, preferred_element_type=jnp.float32)
        * factor
    )
    scores = jnp.where(validity[:, None, None, :] > 0, scores, -1e30)
    highest = jnp.max(scores, axis=-1, keepdims=True)
    expo = jnp.exp(scores - highest)
    probs = expo / jnp.sum(expo, axis=-1, keepdims=True)
    probs_low = probs.astype(jnp.bfloat16)
    attended = jnp.einsum(
        "ghqk,gkhd->gqhd", probs_low, value_heads, preferred_element_type=jnp.float32
    ).astype(jnp.bfloat16)
    dprobs = jnp.einsum(
        "gqhd,gkhd->ghqk", grad_groups, value_heads, preferred_element_type=jnp.float32
    )
    rowdot = jnp.sum(probs * dprobs, axis=-1, keepdims=True)
    dscores = (probs * (dprobs - rowdot) * factor).astype(jnp.bfloat16)
    query_grad = jnp.einsum(
        "ghqk,gkhd->gqhd", dscores, key_heads, preferred_element_type=jnp.float32
    ).astype(jnp.bfloat16)
    return (attended, query_grad)


def cross_attend(queries, prev_pair, own_pairs, prev_validity, validity, cotangent):
    block_count = own_pairs.shape[1]
    width = queries.shape[1]
    heads = width // HD
    query_groups = queries.reshape(block_count, BLOCK, heads, HD)
    grad_groups = cotangent.reshape(block_count, BLOCK, heads, HD)
    first_att, first_grad = attend(
        query_groups[:1], grad_groups[:1], prev_pair[:, None], prev_validity[None]
    )
    rest_att, rest_grad = attend(
        query_groups[1:],
        grad_groups[1:],
        own_pairs[:, : block_count - 1],
        validity[: block_count - 1],
    )
    main_att = jnp.concatenate([first_att, rest_att], 0)
    main_grad = jnp.concatenate([first_grad, rest_grad], 0)
    last_att, last_grad = attend(
        query_groups[:, BLOCK - 1 :], grad_groups[:, BLOCK - 1 :], own_pairs, validity
    )
    main_att = main_att.at[:, BLOCK - 1].set(last_att[:, 0])
    main_grad = main_grad.at[:, BLOCK - 1].set(last_grad[:, 0])
    return (main_att.reshape(-1, width), main_grad.reshape(-1, width))


def on_device(queries, encodings, neighbour_ids, w_key, w_value, cotangent):
    block_count = encodings.shape[1]
    key_count = encodings.shape[2]
    enc_width = encodings.shape[3]
    width = queries.shape[2]
    codes = encodings[0]
    validity = (neighbour_ids[0] != 0).astype(jnp.bfloat16)
    stacked = jnp.stack([w_key, w_value])
    own_pairs = project(codes.reshape(-1, enc_width), stacked).reshape(
        2, block_count, key_count, width
    )
    prev_pair, prev_validity = passed_along(
        (own_pairs[:, block_count - 1], validity[block_count - 1]), "seq", 1
    )
    attended, query_grad = cross_attend(
        queries[0], prev_pair, own_pairs, prev_validity, validity, cotangent[0]
    )
    return (attended[None], query_grad[None])


def solution(mesh):
    return jax.shard_map(
        on_device,
        mesh=mesh,
        in_specs=(
            P("dp", "seq", None),
            P("dp", "seq", None, None),
            P("dp", "seq", None),
            P(None, "dp"),
            P(None, "dp"),
            P("dp", "seq", None),
        ),
        out_specs=(P("dp", "seq", None), P("dp", "seq", None)),
        check_vma=False,
    )
```

profile of v0, /device:TPU:1, one launch (start us, length us, event | category | flops | bytes accessed | tf_op | source)
XLA Modules:
  0.0 848.9 jit_solution(1937294150403743811)
XLA Ops:
  7.2 1.5 pad_maximum_fusion.2
  8.7 0.7 compare_bitcast_fusion
  9.4 12.0 %collective-permute-start.1 = (bf16[256]{0:T(256)(128)(2,1)S(1)}, bf16[256]{0:T(256)(128)(2,1)S(1)}, u32[]{:S(2)}, u32[]{:S(2)}) collective-permute-start(bf16[256]{0:T(256)(128)(2,1)S(1)} %slice_reduce_fusion), channel_id=1, source_target_pairs={{0,1},{1,2},{2,3},{4,5},{5,6},{6,7},{8,9},{9,10},{10,11},{12,13},{... | collective-permute-start | bytes 1544 | tf_op jit(solution)/shard_map/ppermute | solution.py:13
  21.5 1.4 copy.78
  23.0 0.2 copy.75
  23.4 0.8 copy-done.6
  24.3 0.5 copy.28
  24.8 1.1 reshape.289
  26.0 0.9 copy.72
  27.0 0.9 copy.77
  27.9 603.2 %all-gather.2.cloned.1.call-done = bf16[2,448,4096]{1,2,0:T(8,128)(2,1)} async-done(((bf16[2,448,32]{1,2,0:T(8,128)(2,1)}), bf16[2,448,4096]{1,2,0:T(8,128)(2,1)}) %all-gather.2.cloned.1.call-update) | async-done | bytes 7340048 | tf_op jit(solution)/shard_map/all_gather | solution.py:20
  631.1 10.1 %convolution_convert_fusion = bf16[2,4096,512]{1,2,0:T(8,128)(2,1)} fusion(bf16[2,448,4096]{1,2,0:T(8,128)(2,1)} %all-gather.2.cloned.1.call-done, bf16[512,448,1]{0,1,2:T(8,128)(2,1)S(1)} %copy-done.12), kind=kOutput, calls=%fused_computation.7 | convolution fusion | flops 3762290688 | bytes 16187392 | tf_op jit(solution)/shard_map/re,tec->trc/dot_general | solution.py:17
  641.3 5.0 slice.123
  646.2 1.2 copy-done.2
  647.4 2.2 fusion.92
  649.7 6.3 copy.68
  656.0 92.8 %collective-permute-start = (bf16[2,256,4096]{1,2,0:T(8,128)(2,1)}, bf16[2,256,4096]{1,2,0:T(8,128)(2,1)}, u32[]{:S(2)}, u32[]{:S(2)}) collective-permute-start(bf16[2,256,4096]{1,2,0:T(8,128)(2,1)} %bitcast.185), channel_id=1, source_target_pairs={{0,1},{1,2},{2,3},{4,5},{5,6},{6,7},{8,9},{9,10},{10,11},{12,13},{... | collective-permute-start | bytes 12582920 | tf_op jit(solution)/shard_map/ppermute | solution.py:13
  748.9 5.9 slice_bitcast_fusion
  754.8 3.3 copy.70
  758.0 4.1 copy.69
  762.1 5.4 copy.74
  767.5 7.5 copy.65
  775.1 5.6 copy.73
  780.7 0.7 fusion.70
  781.3 0.2 fusion.34
  781.5 4.3 fusion.7
  785.8 1.9 fusion.9
  787.9 0.2 copy-done.1
  788.0 1.2 fusion.63
  789.3 0.5 fusion.57
  789.7 2.0 fusion.94
  791.7 1.8 fusion.53
  793.5 15.5 %fusion.32 = bf16[1,64,32,128]{3,1,2,0:T(8,128)(2,1)} fusion(bf16[256,32,128]{0,2,1:T(8,128)(2,1)S(1)} %bitcast.178, f32[32,256,64]{1,2,0:T(8,128)} %fusion.53, f32[32,64,256]{2,1,0:T(8,128)} %get-tuple-element.39, f32[32,64]{1,0:T(8,128)S(1)} %get-tuple-element.38), kind=kOutput, calls=%fused_computation.43 | convolution fusion | flops 138152192 | bytes 6823936 | tf_op jit(solution)/shard_map/ghqk,gkhd->gqhd/dot_general | solution.py:49
  809.0 3.9 fusion.30
  812.9 2.5 fusion.93
  815.4 1.8 fusion.55
  817.2 0.5 fusion.59
  817.6 1.1 fusion.95
  818.8 1.3 copy-done.13
  820.0 1.7 fusion.29
  821.8 14.7 %fusion.31 = bf16[1,64,32,128]{3,1,2,0:T(8,128)(2,1)S(1)} fusion(bf16[256,32,128]{0,2,1:T(8,128)(2,1)S(1)} %bitcast.182, f32[32,256,64]{1,2,0:T(8,128)} %fusion.55, f32[32,64,256]{2,1,0:T(8,128)} %copy-done.13, f32[32,64]{1,0:T(8,128)S(1)} %get-tuple-element.40), kind=kOutput, calls=%fused_computation.42 | convolution fusion | flops 138152192 | bytes 6823936 | tf_op jit(solution)/shard_map/ghqk,gkhd->gqhd/dot_general | solution.py:49
  836.5 1.1 pad_maximum_fusion
  837.7 0.2 scatter.6
  837.9 0.7 copy.39
  838.5 1.3 broadcast_in_dim_reshape.6
  839.9 0.2 scatter.9
  840.1 0.7 copy.47
  840.8 1.3 broadcast_in_dim_reshape.7
  (44 shorter events, 0.9 us)
Async XLA Ops:
  7.2 15.8 %copy-start.5 = (bf16[1,128,4096]{2,1,0:T(8,128)(2,1)S(1)}, bf16[1,128,4096]{2,1,0:T(8,128)(2,1)}, u32[]{:S(2)}) copy-start(bf16[1,128,4096]{2,1,0:T(8,128)(2,1)} %param.10) | copy-start | bytes 3145732
  7.2 624.0 %all-gather.2.cloned.1.call-start = ((), (), s32[]{:S(2)}) async-start(), calls=%async_computation | async-start | bytes 8454144 | tf_op jit(solution)/shard_map/all_gather | solution.py:20
  9.4 18.5 %collective-permute-start.1 = (bf16[256]{0:T(256)(128)(2,1)S(1)}, bf16[256]{0:T(256)(128)(2,1)S(1)}, u32[]{:S(2)}, u32[]{:S(2)}) collective-permute-start(bf16[256]{0:T(256)(128)(2,1)S(1)} %slice_reduce_fusion), channel_id=1, source_target_pairs={{0,1},{1,2},{2,3},{4,5},{5,6},{6,7},{8,9},{9,10},{10,11},{12,13},{... | collective-permute-start | bytes 1544 | tf_op jit(solution)/shard_map/ppermute | solution.py:13
  22.9 1.2 copy-start.6
  23.2 1.1 copy-start.11
  26.0 605.2 %copy-start.12 = (bf16[512,448,1]{0,1,2:T(8,128)(2,1)S(1)}, bf16[512,448,1]{0,1,2:T(8,128)(2,1)}, u32[]{:S(2)}) copy-start(bf16[512,448,1]{0,1,2:T(8,128)(2,1)} %reshape.289) | copy-start | bytes 1376260
  641.3 6.2 copy-start.2
  656.0 156.9 %collective-permute-start = (bf16[2,256,4096]{1,2,0:T(8,128)(2,1)}, bf16[2,256,4096]{1,2,0:T(8,128)(2,1)}, u32[]{:S(2)}, u32[]{:S(2)}) collective-permute-start(bf16[2,256,4096]{1,2,0:T(8,128)(2,1)} %bitcast.185), channel_id=1, source_target_pairs={{0,1},{1,2},{2,3},{4,5},{5,6},{6,7},{8,9},{9,10},{10,11},{12,13},{... | collective-permute-start | bytes 12582920 | tf_op jit(solution)/shard_map/ppermute | solution.py:13
  775.1 5.6 copy-start
  781.5 4.3 copy-start.4
  785.8 2.2 copy-start.1
  788.0 1.2 copy-start.8
  789.7 2.0 copy-start.3
  789.7 2.0 copy-start.7
  818.7 1.3 copy-start.13
  821.8 14.7 %copy-start.10 = (bf16[1,64,32,128]{3,1,2,0:T(8,128)(2,1)S(1)}, bf16[1,64,32,128]{3,1,2,0:T(8,128)(2,1)}, u32[]{:S(2)}) copy-start(bf16[1,64,32,128]{3,1,2,0:T(8,128)(2,1)} %fusion.30) | copy-start | bytes 1572868
  837.8 2.0 copy-start.9
Sparse Core Ops, SparseCore 0:
  10.1 620.9 all-gather.1
where the time goes:
time: 856 us; the launch traced here: 849 us
  waiting for transfers between devices  603 us (70%)
  starting transfers between devices  105 us (12%)
  local copies, waits for them, and re-layouts  61.2 us (7%)
  matrix products  58.4 us (7%)
  between operations  14.3 us (2%)
    all_gather x1, waiting for transfers between devices, project(): lax.all_gather(stacked, 'dp', axis=2, tiled=True)  603 us
    ppermute x2, starting transfers between devices, passed_along(): return lax.ppermute(block, axis, route)  105 us
    unnamed x43, local copies, waits for them, and re-layouts  38.5 us
    dot_general x3, matrix products, attend(): jnp.einsum('ghqk,gkhd->gqhd', dscores, key_heads, preferred_element_type=...  31.4 us
  transfers between devices with their start and end apart: 3, of which 1 were waited for; matrix products, arithmetic and copies ran while one was open for 8% of the time, Pallas kernels for 0%

commit v1 on v0

v1 whole, which is shorter than its diff:
```python
import jax
import jax.numpy as jnp
from jax import lax
from jax.experimental import pallas as pl
from jax.experimental.pallas import tpu as pltpu
from jax.sharding import PartitionSpec as P

HD = 128
ENC = 448
BLOCK = 64
KEYS = 256
WIDTH = 4096
HALF = WIDTH // 2
PIECE = 32
GROUPS = 5
SHIFTED = 272
FACTOR = HD ** -0.5
EXPONENT = FACTOR * 1.4426950408889634
MASKED = -1e30
NT = (((1,), (1,)), ((), ()))
NN = (((1,), (0,)), ((), ()))
MESH = pl.DeviceIdType.MESH
GROUP_ROWS = tuple((BLOCK * g, BLOCK if g < 4 else 16) for g in range(GROUPS))
CHUNK = 32

ORDER = (
    tuple((d, i) for d in (0, 1, 3, 2) for i in range(4)),
    tuple((0, i) for i in range(4))
    + ((1, 0), (3, 0), (1, 1), (3, 1), (2, 0), (2, 1), (1, 2), (1, 3), (3, 2), (3, 3), (2, 2), (2, 3)),
)
PAIRS = (
    ((0, 0), (0, 1), (1, 0), (1, 1), (3, 0), (3, 1), (2, 0), (2, 1)),
    ((0, 0), (0, 1), (1, 0), (3, 0), (2, 0), (1, 1), (3, 1), (2, 1)),
)


def dot(a, b, dims):
    return lax.dot_general(a, b, dims, preferred_element_type=jnp.float32)


def pick(core, first, second):
    return first + core * (second - first)


def table(step, values):
    out = jnp.int32(values[0])
    for i, v in enumerate(values[1:], 1):
        out = jnp.where(step == i, jnp.int32(v), out)
    return out


def softmax_parts(s, dp, bias):
    s = s + bias
    top = jnp.max(s, axis=1, keepdims=True)
    e = jnp.exp2((s - top) * EXPONENT)
    p = e * (1.0 / jnp.sum(e, axis=1, keepdims=True))
    rowdot = jnp.sum(p * dp, axis=1, keepdims=True)
    return p.astype(jnp.bfloat16), ((p * FACTOR) * (dp - rowdot)).astype(jnp.bfloat16)


def kernel(
    q_hbm, ct_hbm, e_hbm, ids_hbm, wk_ref, wv_ref, att_hbm, gr_hbm,
    w, qraw, ctraw, qs, cts, eraw, e1, e2, ids, kb, vb, sbuf, dbuf, pbuf, dsbuf, attbuf, grbuf,
    in_sem, in_send, in_recv, prev_send, prev_recv, y_send, y_recv, a_send, a_recv, b_send, b_recv,
    f_send, f_recv, out_sem, out_send, out_recv,
):
    dp, seq = lax.axis_index("dp"), lax.axis_index("seq")
    y, zl, x = lax.div(dp, 16), lax.rem(lax.div(dp, 4), 4), lax.rem(dp, 4)
    z_hi, core = lax.div(seq, 2), lax.rem(seq, 2)
    z = z_hi * 4 + zl
    other = 1 - core
    a_me, b_me = pick(core, zl, x), pick(core, x, zl)

    def device(dy=0, dz=0, dx=0, to_core=None):
        yy, zz, xx = lax.rem(y + dy + 8, 8), lax.rem(z + dz + 8, 8), lax.rem(x + dx + 4, 4)
        return (yy * 16 + lax.rem(zz, 4) * 4 + xx, lax.div(zz, 4) * 2 + (core if to_core is None else to_core))

    def along_a(d):
        return device(dz=d * other, dx=d * core)

    def along_b(d):
        return device(dz=d * core, dx=d * other)

    sibling = device(to_core=other)

    def remote(src, dst, send, recv, to):
        return pltpu.make_async_remote_copy(
            src_ref=src, dst_ref=dst, send_sem=send, recv_sem=recv, device_id=to, device_id_type=MESH
        )

    def piece(yi, a, b):
        a, b = lax.rem(a, 4), lax.rem(b, 4)
        return w.at[pick(core, a, b) * 4 + yi, pick(core, b, a)]

    barrier = pltpu.get_barrier_semaphore()
    peers = [device(dy=d) for d in range(1, 8)] + [device(dx=d) for d in (1, 2, 3)]
    peers += [device(dz=d) for d in (1, 2, -1, -2)] + [sibling]
    peers += [device(dz=4), device(dz=4, to_core=other)]
    for peer in peers:
        pl.semaphore_signal(barrier, inc=1, device_id=peer, device_id_type=MESH)

    eye = (
        lax.broadcasted_iota(jnp.int32, (PIECE, PIECE), 0) == lax.broadcasted_iota(jnp.int32, (PIECE, PIECE), 1)
    ).astype(jnp.float32).astype(jnp.bfloat16)
    gap = jnp.zeros((512 - ENC, PIECE), jnp.bfloat16)
    left = dot(eye, jnp.concatenate([wk_ref[...], gap], 0), NT)
    right = dot(eye, jnp.concatenate([gap, wv_ref[...]], 0), NT)
    mine = w.at[zl * 4 + lax.div(y, 2), x]
    is_source = lax.rem(y, 2) == core

    @pl.when(is_source)
    def _():
        mine[:, 0:384] = left[:, 0:384].astype(jnp.bfloat16)
        mine[:, 384:512] = (left[:, 384:512] + right[:, 0:128]).astype(jnp.bfloat16)
        mine[:, 512:896] = right[:, 128:512].astype(jnp.bfloat16)

    pl.semaphore_wait(barrier, len(peers))

    def y_copy(d):
        return remote(mine, mine, y_send.at[d - 1], y_recv.at[lax.div(y, 2)], device(dy=d))

    @pl.when(is_source)
    def _():
        for d in (1, 7, 2, 6, 3, 5, 4):
            y_copy(d).start()

    def prev_copies():
        return [
            remote(
                e_hbm.at[0, 1, pl.ds(128 * t, 128)], eraw.at[0, pl.ds(128 * t, 128)],
                prev_send.at[t], prev_recv.at[0], device(dz=4, to_core=t),
            )
            for t in range(2)
        ] + [
            remote(ids_hbm.at[0], ids.at[0], prev_send.at[2 + t], prev_recv.at[1], device(dz=4, to_core=t))
            for t in range(2)
        ]

    gives_prev = jnp.logical_and(z_hi == 0, core == 1)

    @pl.when(gives_prev)
    def _():
        for copy in prev_copies():
            copy.start()

    rows = pl.ds(pl.multiple_of(core * 128, 128), 128)
    locals_, sends = [], []
    for n, (src, dst) in enumerate(((q_hbm, qraw), (ct_hbm, ctraw))):
        for i in range(4):
            own = pl.ds(pl.multiple_of(i * 1024 + core * 512, 512), 512)
            his = pl.ds(pl.multiple_of(i * 1024 + other * 512, 512), 512)
            to = dst.at[rows, pl.ds(i * 512, 512)]
            locals_.append(pltpu.make_async_copy(src.at[0, :, own], to, in_sem.at[n * 4 + i]))
            sends.append(remote(src.at[0, :, his], to, in_send.at[n * 4 + i], in_recv.at[n * 4 + i], sibling))
    mine_e = eraw.at[pl.ds(1 + 2 * core, 2)]
    locals_.append(pltpu.make_async_copy(e_hbm.at[0], mine_e, in_sem.at[8]))
    sends.append(remote(e_hbm.at[0], mine_e, in_send.at[8], in_recv.at[8], sibling))
    mine_ids = ids.at[1 + core]
    locals_.append(pltpu.make_async_copy(ids_hbm.at[0], mine_ids, in_sem.at[9]))
    sends.append(remote(ids_hbm.at[0], mine_ids, in_send.at[9], in_recv.at[9], sibling))
    for copy in locals_ + sends:
        copy.start()

    def in_wait(n):
        his_rows = pl.ds(pl.multiple_of(other * 128, 128), 128)
        if n < 8:
            buf = (qraw, ctraw)[n // 4]
            to = buf.at[his_rows, pl.ds((n % 4) * 512, 512)]
        elif n == 8:
            to = eraw.at[pl.ds(1 + 2 * other, 2)]
        else:
            to = ids.at[1 + other]
        locals_[n].wait()
        remote(to, to, in_send.at[n], in_recv.at[n], sibling).wait_recv()

    def shift(n, raw, out):
        for i in range(4):
            in_wait(n * 4 + i)

        def body(j, carry):
            cols = pl.ds(pl.multiple_of(j * 256, 256), 256)
            moved = pltpu.roll(raw[:, cols].astype(jnp.float32), 1, 0).astype(jnp.bfloat16)
            out[0:256, cols] = moved
            out[256:272, cols] = moved[0:16]
            return carry

        lax.fori_loop(0, 8, body, 0)

    shift(0, qraw, qs)
    shift(1, ctraw, cts)

    def a_copy(yi, d):
        here = piece(yi, a_me, b_me)
        far = 2 if yi % 2 == 0 else -2
        offset = {1: 1, 3: -1, 2: far}[d]
        return remote(here, here, a_send.at[yi * 3 + d - 1], a_recv.at[(4 - d) * 4 + yi], along_a(offset))

    def b_copy(da, yi, side):
        here = piece(yi, a_me + da, b_me)
        at = da * 4 + yi
        return remote(here, here, b_send.at[side * 16 + at], b_recv.at[side * 16 + at], along_b(1 - 2 * side))

    def entry(n):
        (d0, y0), (d1, y1) = ORDER[0][n], ORDER[1][n]
        return pick(core, d0, d1), pick(core, y0, y1)

    for yi in range(4):
        @pl.when(2 * yi + core != y)
        def _():
            here = piece(yi, a_me, b_me)
            remote(here, here, y_send.at[0], y_recv.at[yi], device(dy=1)).wait_recv()

        for d in (1, 3, 2):
            a_copy(yi, d).start()
        for side in range(2):
            b_copy(0, yi, side).start()

    r0 = lax.broadcasted_iota(jnp.int32, (ENC, 512), 0)
    r1 = lax.broadcasted_iota(jnp.int32, (ENC, 512), 1)
    place1 = (r0 == r1).astype(jnp.float32).astype(jnp.bfloat16)
    place2 = (r0 + (512 - ENC) == r1).astype(jnp.float32).astype(jnp.bfloat16)

    def pad(slot):
        block = eraw[slot]
        e1[pl.ds(slot * KEYS, KEYS), :] = dot(block, place1, NN).astype(jnp.bfloat16)
        e2[pl.ds(slot * KEYS, KEYS), :] = dot(block, place2, NN).astype(jnp.bfloat16)

    in_wait(8)
    in_wait(9)
    for slot in range(1, GROUPS):
        pad(slot)

    def a_arrived(n):
        da, yi = entry(n)
        there = piece(yi, a_me + da, b_me)
        remote(there, there, a_send.at[0], a_recv.at[da * 4 + yi], along_a(1)).wait_recv()
        for side in range(2):
            b_copy(da, yi, side).start()

    def forward(n, side):
        da, yi = entry(n)
        at = da * 4 + yi
        there = piece(yi, a_me + da, b_me + (3 if side == 0 else 1))
        half = there.at[pl.ds(16 * side, 16)]
        return there, at, remote(
            half, half, f_send.at[side * 16 + at], f_recv.at[side * 16 + at], along_b(1 - 2 * side)
        )

    def pass_on(first, last):
        for n in range(first, last):
            for side in range(2):
                there, at, copy = forward(n, side)
                remote(there, there, b_send.at[0], b_recv.at[side * 16 + at], along_b(1)).wait_recv()
                copy.start()

    def passed(first, last):
        for n in range(first, last):
            da, yi = entry(n)
            at = da * 4 + yi
            there = piece(yi, a_me + da, b_me + 2)
            for side in range(2):
                half = there.at[pl.ds(16 * side, 16)]
                remote(half, half, f_send.at[0], f_recv.at[side * 16 + at], along_b(1)).wait_recv()

    for n in range(4, 8):
        a_arrived(n)
    pass_on(0, 4)

    def prev_on():
        half = eraw.at[0, pl.ds(pl.multiple_of(core * 128, 128), 128)]
        return remote(half, half, prev_send.at[4], prev_recv.at[2], sibling)

    @pl.when(z_hi == 1)
    def _():
        half = eraw.at[0, pl.ds(pl.multiple_of(core * 128, 128), 128)]
        remote(half, half, prev_send.at[0], prev_recv.at[0], sibling).wait_recv()
        remote(ids.at[0], ids.at[0], prev_send.at[2], prev_recv.at[1], sibling).wait_recv()
        prev_on().start()

    @pl.when(z_hi == 0)
    def _():
        eraw[0] = jnp.zeros((KEYS, ENC), jnp.bfloat16)
        ids[0] = jnp.zeros((2, KEYS), jnp.int32)

    for n in range(8, 16):
        a_arrived(n)

    @pl.when(z_hi == 1)
    def _():
        half = eraw.at[0, pl.ds(pl.multiple_of(other * 128, 128), 128)]
        remote(half, half, prev_send.at[4], prev_recv.at[2], sibling).wait_recv()

    pad(0)

    def out_copies(step, head, col, out_col):
        found = []
        for n, (buf, out) in enumerate(((attbuf, att_hbm), (grbuf, gr_hbm))):
            at = (step * 2 + head) * 2 + n
            src = buf.at[pl.ds(pl.multiple_of(other * 128, 128), 128), col]
            found.append(remote(src, out.at[:, out_col], out_send.at[at], out_recv.at[at], sibling))
            found.append(pltpu.make_async_copy(buf.at[rows, col], out.at[:, out_col], out_sem.at[at]))
        return found

    def columns(step, head, of_core):
        dz = jnp.where(of_core == 0, table(step, [p[0] for p in PAIRS[0]]), table(step, [p[0] for p in PAIRS[1]]))
        yp = jnp.where(of_core == 0, table(step, [p[1] for p in PAIRS[0]]), table(step, [p[1] for p in PAIRS[1]]))
        zz, yi = lax.rem(zl + dz, 4), yp * 2 + head
        col = pl.ds(pl.multiple_of((yi * 4 + zz) * HD, HD), HD)
        out_col = pl.ds(pl.multiple_of((yi * 8 + of_core * 4 + zz) * HD, HD), HD)
        return zz * 4 + yi, col, out_col

    def work(step, carry):
        @pl.when(step == 0)
        def _():
            passed(0, 4)

        @pl.when(step == 1)
        def _():
            pass_on(4, 8)

        @pl.when(step == 2)
        def _():
            pass_on(8, 12)
            passed(4, 8)

        @pl.when(step == 3)
        def _():
            pass_on(12, 16)

        @pl.when(step == 4)
        def _():
            passed(8, 12)

        @pl.when(step == 6)
        def _():
            passed(12, 16)

        first = columns(step, 0, core)[0]
        cols = [columns(step, h, core)[1] for h in range(2)]
        wt = w[pl.ds(first, 2)].reshape(2 * HD, 2 * ENC)
        kb[...] = dot(e1[...], wt[:, 0:512], NT).astype(jnp.bfloat16)
        vb[...] = dot(e2[...], wt[:, 384:896], NT).astype(jnp.bfloat16)
        for h in range(2):
            hs = slice(h * HD, h * HD + HD)
            for g, (r, m) in enumerate(GROUP_ROWS):
                ks = slice(KEYS * g, KEYS * g + KEYS)
                sbuf[h, r:r + m] = dot(qs[r:r + m, cols[h]], kb[ks, hs], NT)
                dbuf[h, r:r + m] = dot(cts[r:r + m, cols[h]], vb[ks, hs], NT)
        for h in range(2):
            for g, (r, m) in enumerate(GROUP_ROWS):
                bias = jnp.where(ids[(g + 1) // 2, (g + 1) % 2:(g + 1) % 2 + 1, :] != 0, 0.0, MASKED)
                for c0 in range(r, r + m, CHUNK):
                    c1 = min(c0 + CHUNK, r + m)
                    pbuf[h, c0:c1], dsbuf[h, c0:c1] = softmax_parts(sbuf[h, c0:c1], dbuf[h, c0:c1], bias)
        for h in range(2):
            hs = slice(h * HD, h * HD + HD)
            for buf, weights, other_side in ((attbuf, pbuf, vb), (grbuf, dsbuf, kb)):
                parts = [
                    dot(weights[h, r:r + m], other_side[KEYS * g:KEYS * g + KEYS, hs], NN)
                    for g, (r, m) in enumerate(GROUP_ROWS)
                ]
                moved = pltpu.roll(jnp.concatenate(parts, 0), SHIFTED - 1, 0)
                buf[:, cols[h]] = moved[0:256].astype(jnp.bfloat16)
        for h in range(2):
            _, col, out_col = columns(step, h, core)
            for copy in out_copies(step, h, col, out_col):
                copy.start()
        return carry

    lax.fori_loop(0, 8, work, 0)

    def finish(step, carry):
        for h in range(2):
            _, col, out_col = columns(step, h, core)
            _, _, his_col = columns(step, h, other)
            for n, copy in enumerate(out_copies(step, h, col, out_col)):
                if n % 2:
                    copy.wait()
                else:
                    copy.wait_send()
                    out = (att_hbm, gr_hbm)[n // 2]
                    at = (step * 2 + h) * 2 + n // 2
                    there = out.at[:, his_col]
                    remote(there, there, out_send.at[at], out_recv.at[at], sibling).wait_recv()
        return carry

    lax.fori_loop(0, 8, finish, 0)
    for copy in sends:
        copy.wait_send()

    @pl.when(is_source)
    def _():
        for d in range(1, 8):
            y_copy(d).wait_send()

    for yi in range(4):
        for d in (1, 2, 3):
            a_copy(yi, d).wait_send()
    for n in range(16):
        da, yi = entry(n)
        for side in range(2):
            b_copy(da, yi, side).wait_send()
            forward(n, side)[2].wait_send()

    @pl.when(gives_prev)
    def _():
        for copy in prev_copies():
            copy.wait_send()

    @pl.when(z_hi == 1)
    def _():
        prev_on().wait_send()


def on_device(queries, encodings, neighbour_ids, w_key, w_value, cotangent):
    bf16, f32, dma = jnp.bfloat16, jnp.float32, pltpu.SemaphoreType.DMA
    whole, anywhere = pl.BlockSpec(memory_space=pltpu.VMEM), pl.BlockSpec(memory_space=pl.ANY)
    attended, query_grad = pl.pallas_call(
        kernel,
        out_shape=(jax.ShapeDtypeStruct((128, WIDTH), bf16),) * 2,
        in_specs=[anywhere] * 4 + [whole] * 2,
        out_specs=(anywhere,) * 2,
        scratch_shapes=[
            pltpu.VMEM((16, 4, PIECE, 2 * ENC), bf16),
            pltpu.VMEM((256, HALF), bf16),
            pltpu.VMEM((256, HALF), bf16),
            pltpu.VMEM((SHIFTED, HALF), bf16),
            pltpu.VMEM((SHIFTED, HALF), bf16),
            pltpu.VMEM((GROUPS, KEYS, ENC), bf16),
            pltpu.VMEM((GROUPS * KEYS, 512), bf16),
            pltpu.VMEM((GROUPS * KEYS, 512), bf16),
            pltpu.VMEM((3, 2, KEYS), jnp.int32),
            pltpu.VMEM((GROUPS * KEYS, 2 * HD), bf16),
            pltpu.VMEM((GROUPS * KEYS, 2 * HD), bf16),
            pltpu.VMEM((2, SHIFTED, KEYS), f32),
            pltpu.VMEM((2, SHIFTED, KEYS), f32),
            pltpu.VMEM((2, SHIFTED, KEYS), bf16),
            pltpu.VMEM((2, SHIFTED, KEYS), bf16),
            pltpu.VMEM((256, HALF), bf16),
            pltpu.VMEM((256, HALF), bf16),
            dma((10,)), dma((10,)), dma((10,)),
            dma((5,)), dma((3,)),
            dma((7,)), dma((4,)),
            dma((12,)), dma((16,)),
            dma((32,)), dma((32,)),
            dma((32,)), dma((32,)),
            dma((32,)), dma((32,)), dma((32,)),
        ],
        compiler_params=pltpu.CompilerParams(
            collective_id=0, has_side_effects=True, vmem_limit_bytes=40 << 20
        ),
    )(queries, cotangent, encodings, neighbour_ids, w_key, w_value)
    return attended[None], query_grad[None]


def solution(mesh):
    return jax.shard_map(
        on_device,
        mesh=mesh,
        in_specs=(
            P("dp", "seq", None),
            P("dp", "seq", None, None),
            P("dp", "seq", None),
            P(None, "dp"),
            P(None, "dp"),
            P("dp", "seq", None),
        ),
        out_specs=(P("dp", "seq", None), P("dp", "seq", None)),
        check_vma=False,
    )
```

time: 856 us -> 62.5 us (0.07)
  waiting for transfers between devices: 603 us -> 0 us
  starting transfers between devices: 105 us -> 0 us
  matrix products: 58.4 us -> 0 us
  Pallas kernels: 0 us -> 56.1 us
  local copies, waits for them, and re-layouts: 61.2 us -> 5.53 us
  between operations: 14.3 us -> 0.7 us
    all_gather x1 -> x0, waiting for transfers between devices: 603 us -> none  [project(): lax.all_gather(stacked, 'dp', axis=2, tiled=True)]
    ppermute x2 -> x0, starting transfers between devices: 105 us -> none  [passed_along(): return lax.ppermute(block, axis, route)]
    dot_general x13 -> x0, matrix products: 58.4 us -> none  [the longest x3 31.4 us: attend(): jnp.einsum('ghqk,gkhd->gqhd', dscores, key_heads, preferred_element_type=...]
    pallas_call x0 -> x1, Pallas kernels: none -> 56.1 us  [on_device(): pl.pallas_call(kernel, out_shape=(jax.ShapeDtypeStruct((128, WIDTH), bf16...]
    unnamed x43 -> x13, local copies, waits for them, and re-layouts: 38.5 us -> 5.53 us
    another operation x6 -> x0, local copies, waits for them, and re-layouts: 11.1 us -> none  [the longest x1 7.52 us: attend(): key_heads = pairs[0].reshape(groups, key_count, heads, HD)]
    slice x4 -> x0, local copies, waits for them, and re-layouts: 9.73 us -> none  [the longest x1 4.97 us: on_device(): own_pairs[:, block_count - 1]]
  transfers between devices with their start and end apart: 3 -> 0, of which waited for: 1 -> 0; matrix products, arithmetic and copies ran while one was open for 8% -> 0% of each run, Pallas kernels for 0% -> 0%
where the time goes in v1:
time: 62.5 us; the launch traced here: 62.3 us
  Pallas kernels  56.1 us (90%)
  local copies, waits for them, and re-layouts  5.53 us (9%)
  between operations  0.7 us (1%)
    pallas_call x1, Pallas kernels, on_device(): pl.pallas_call(kernel, out_shape=(jax.ShapeDtypeStruct((128, WIDTH), bf16...  56.1 us
    unnamed x13, local copies, waits for them, and re-layouts  5.53 us

profile of v1, /device:TPU:1, one launch (start us, length us, event | category | flops | bytes accessed | tf_op | source)
XLA Modules:
  0.0 62.3 jit_solution(8594246093845997222)
XLA Ops:
  0.6 0.0 copy-start.3
  0.6 0.0 copy-start
  0.6 1.0 %copy.9.wk_ref = bf16[448,32]{1,0:T(8,128)(2,1)S(1)} copy(bf16[448,32]{0,1:T(8,128)(2,1)} %param.9) | data formatting | bytes 57344 | tf_op args[3]
  1.6 0.0 copy-done.3
  1.6 0.1 copy.10.wv_ref
  1.8 0.0 copy-start.2
  1.8 1.2 %copy.8.e_hbm = bf16[1,2,256,448]{3,2,1,0:T(8,128)(2,1)S(1)} copy(bf16[1,2,256,448]{2,3,1,0:T(8,128)(2,1)} %param.7) | data formatting | bytes 917504 | tf_op args[1]
  3.0 0.0 copy-done
  3.0 0.0 copy-done.2
  3.1 0.0 copy-start.1
  3.1 1.2 %copy-done.1 = bf16[1,128,4096]{2,1,0:T(8,128)(2,1)S(1)} copy-done((bf16[1,128,4096]{2,1,0:T(8,128)(2,1)S(1)}, bf16[1,128,4096]{2,1,0:T(8,128)(2,1)}, u32[]{:S(2)}) %copy-start.1) | copy-done | bytes 1048600
  4.3 56.1 %shard_map.77 = (bf16[128,4096]{1,0:T(8,128)(2,1)S(1)}, bf16[128,4096]{1,0:T(8,128)(2,1)S(1)}) custom-call(bf16[1,128,4096]{2,1,0:T(8,128)(2,1)S(1)} %copy-done, bf16[1,128,4096]{2,1,0:T(8,128)(2,1)S(1)} %copy-done.1, bf16[1,2,256,448]{3,2,1,0:T(8,128)(2,1)S(1)} %copy.8.e_hbm, s32[1,2,256]{2,1,0:T(2,128)S(1)} %copy-done.2, bf16[448,32]{1,0:T(8,128)(2,1)S(1)} %copy.9.wk_ref, ...), custom_call_target="tpu_custom_call" | custom-call | tf_op jit(solution)/shard_map/pallas_call | solution.py:418
  60.3 1.0 %copy.13 = bf16[1,128,4096]{2,1,0:T(8,128)(2,1)} copy(bf16[1,128,4096]{2,1,0:T(8,128)(2,1)S(1)} %bitcast.3) | data formatting | bytes 2097152
  61.3 1.0 %copy.14 = bf16[1,128,4096]{2,1,0:T(8,128)(2,1)} copy(bf16[1,128,4096]{2,1,0:T(8,128)(2,1)S(1)} %bitcast.2) | data formatting | bytes 2097152
Async XLA Ops:
  0.6 1.0 %copy-start.3 = (bf16[448,32]{0,1:T(8,128)(2,1)S(1)}, bf16[448,32]{0,1:T(8,128)(2,1)}, u32[]{:S(2)}) copy-start(bf16[448,32]{0,1:T(8,128)(2,1)} %param.10) | copy-start | bytes 86020
  0.6 2.4 %copy-start = (bf16[1,128,4096]{2,1,0:T(8,128)(2,1)S(1)}, bf16[1,128,4096]{2,1,0:T(8,128)(2,1)}, u32[]{:S(2)}) copy-start(bf16[1,128,4096]{2,1,0:T(8,128)(2,1)} %q_hbm.1) | copy-start | bytes 3145732
  1.8 1.3 %copy-start.2 = (s32[1,2,256]{2,1,0:T(2,128)S(1)}, s32[1,2,256]{2,1,0:T(2,128)}, u32[]{:S(2)}) copy-start(s32[1,2,256]{2,1,0:T(2,128)} %ids_hbm.1) | copy-start | bytes 6148
  3.1 1.2 %copy-start.1 = (bf16[1,128,4096]{2,1,0:T(8,128)(2,1)S(1)}, bf16[1,128,4096]{2,1,0:T(8,128)(2,1)}, u32[]{:S(2)}) copy-start(bf16[1,128,4096]{2,1,0:T(8,128)(2,1)} %ct_hbm.1) | copy-start | bytes 3145732

commit v2 on v1

v2 whole, which is shorter than its diff:
```python
import jax
import jax.numpy as jnp
from jax import lax
from jax.experimental import pallas as pl
from jax.experimental.pallas import tpu as pltpu
from jax.sharding import PartitionSpec as P

HD = 128
ENC = 448
BLOCK = 64
KEYS = 256
WIDTH = 4096
HALF = WIDTH // 2
PIECE = 32
GROUPS = 5
SHIFTED = 272
FACTOR = HD ** -0.5
EXPONENT = FACTOR * 1.4426950408889634
MASKED = -1e30
NT = (((1,), (1,)), ((), ()))
NN = (((1,), (0,)), ((), ()))
TN = (((0,), (0,)), ((), ()))
MESH = pl.DeviceIdType.MESH
GROUP_ROWS = tuple((BLOCK * g, BLOCK if g < 4 else 16) for g in range(GROUPS))
CHUNK = 32

ROWS = (0, 1, -1, -2, 2, 3, -3, 4)


def dot(a, b, dims):
    return lax.dot_general(a, b, dims, preferred_element_type=jnp.float32)


def pick(core, first, second):
    return first + core * (second - first)


def softmax_parts(s, dp, bias):
    s = s + bias
    top = jnp.max(s, axis=1, keepdims=True)
    e = jnp.exp2((s - top) * EXPONENT)
    p = e * (1.0 / jnp.sum(e, axis=1, keepdims=True))
    rowdot = jnp.sum(p * dp, axis=1, keepdims=True)
    return p.astype(jnp.bfloat16), ((p * FACTOR) * (dp - rowdot)).astype(jnp.bfloat16)


def kernel(
    q_hbm, ct_hbm, e_hbm, ids_hbm, wk_ref, wv_ref, att_hbm, gr_hbm,
    w, qraw, ctraw, qs, cts, eraw, e1, e2, ids, kb, vb, sbuf, dbuf, pbuf, dsbuf, attbuf, grbuf,
    ready, in_sem, in_send, in_recv, prev_send, prev_recv, first_send, first_recv, z_send, z_recv,
    last_send, last_recv, out_sem, out_send, out_recv,
):
    dp, seq = lax.axis_index("dp"), lax.axis_index("seq")
    y, zl, x = lax.div(dp, 16), lax.rem(lax.div(dp, 4), 4), lax.rem(dp, 4)
    z_hi, core = lax.div(seq, 2), lax.rem(seq, 2)
    other = 1 - core
    zi_me = lax.div(zl, 2)
    is_source = lax.rem(zl, 2) == core
    turn = 1 - 2 * lax.rem(y, 2)
    z = z_hi * 4 + zl
    barrier = pltpu.get_barrier_semaphore()

    def place(axis, t):
        yy = lax.rem(y + t, 8) if axis == "y" else y
        zz = z_hi * 4 + lax.rem(zl + t, 4) if axis == "z" else z
        xx = lax.rem(x + t, 4) if axis == "x" else x
        return yy, zz, xx

    def peer(axis, t):
        yy, zz, xx = place(axis, t)
        return (yy * 16 + lax.rem(zz, 4) * 4 + xx, lax.div(zz, 4) * 2 + core)

    def rank(axis, yy, zz, xx):
        key = {"y": jnp.where(yy < 4, yy, 11 - yy), "x": jnp.where(xx < 2, xx, 5 - xx)}.get(axis, zz)
        return jnp.where(yy + zz + xx == 0, 99, key)

    def later(axis, t):
        return rank(axis, *place(axis, t)) > rank(axis, y, z, x)

    def slot(axis, t):
        return {"y": 0, "x": 7, "z": 10}[axis] + t - 1

    sizes = {"y": 8, "x": 4, "z": 4}
    sibling = (dp, z_hi * 2 + other)
    source1 = jnp.logical_and(is_source, core == 1)

    edges = [("z", t, True) for t in range(1, 4)] + [("x", t, core == 0) for t in (1, 3)]
    edges += [("y", t, True) for t in (1, 7)]
    gives_prev = jnp.logical_and(z_hi == 0, core == 1)
    count = 1 + jnp.where(z_hi == 1, 1, 0) + jnp.where(source1, 3, 0)

    @pl.when(source1)
    def _():
        for t in (2, 1, 3):
            pl.semaphore_signal(barrier, inc=1, device_id=peer("x", t), device_id_type=MESH)

    for axis, t, active in edges:
        after = jnp.logical_and(active, later(axis, t))
        before = jnp.logical_and(active, jnp.logical_not(later(axis, t)))
        count = count + jnp.where(before, 1, 0)

        @pl.when(after)
        def _():
            pl.semaphore_signal(barrier, inc=1, device_id=peer(axis, t), device_id_type=MESH)

    pl.semaphore_signal(barrier, inc=1, device_id=sibling, device_id_type=MESH)

    @pl.when(gives_prev)
    def _():
        for t in range(2):
            pl.semaphore_signal(barrier, inc=1, device_id=(dp, 2 + t), device_id_type=MESH)

    r0 = lax.broadcasted_iota(jnp.int32, (ENC, 512), 0)
    r1 = lax.broadcasted_iota(jnp.int32, (ENC, 512), 1)
    place1 = (r0 == r1).astype(jnp.float32).astype(jnp.bfloat16)
    place2 = (r0 + (512 - ENC) == r1).astype(jnp.float32).astype(jnp.bfloat16)
    left = dot(wk_ref[...], place1, NN)
    right = dot(wv_ref[...], place2, NN)

    def piece(zi, yy, xx):
        return w.at[lax.rem(yy + 16, 8) * 2 + zi, lax.rem(xx + 8, 4)]

    mine = piece(zi_me, y, x)

    @pl.when(is_source)
    def _():
        mine[:, 0:384] = left[:, 0:384].astype(jnp.bfloat16)
        mine[:, 384:512] = (left[:, 384:512] + right[:, 0:128]).astype(jnp.bfloat16)
        mine[:, 512:896] = right[:, 128:512].astype(jnp.bfloat16)

    def remote(src, dst, send, recv, to):
        return pltpu.make_async_remote_copy(
            src_ref=src, dst_ref=dst, send_sem=send, recv_sem=recv, device_id=to, device_id_type=MESH
        )

    def first_copy(axis, t):
        back = sizes[axis] - t
        return remote(mine, mine, first_send.at[t - 1], first_recv.at[back - 1], peer(axis, t))

    pl.semaphore_wait(barrier, count)

    @pl.when(source1)
    def _():
        for t in (2, 1, 3):
            first_copy("x", t).start()

    for axis, t, active in edges:
        before = jnp.logical_and(active, jnp.logical_not(later(axis, t)))

        @pl.when(before)
        def _():
            pl.semaphore_signal(
                ready.at[slot(axis, sizes[axis] - t)], inc=1, device_id=peer(axis, t), device_id_type=MESH
            )

    @pl.when(z_hi == 1)
    def _():
        pl.semaphore_signal(ready.at[13 + core], inc=1, device_id=(dp, 1), device_id_type=MESH)

    def ensure(axis, t):
        @pl.when(later(axis, t))
        def _():
            pl.semaphore_wait(ready.at[slot(axis, t)], 1)

    def first_wait(axis, t, there):
        remote(there, there, first_send.at[0], first_recv.at[t - 1], peer(axis, 1)).wait_recv()

    def z_copy(i, t, here):
        return remote(here, here, z_send.at[i * 3 + t - 1], z_recv.at[zi_me * 8 + i], peer("z", t))

    def z_wait(zi, i, there):
        remote(there, there, z_send.at[0], z_recv.at[zi * 8 + i], peer("z", 1)).wait_recv()

    rows = pl.ds(pl.multiple_of(core * 128, 128), 128)
    his_rows = pl.ds(pl.multiple_of(other * 128, 128), 128)

    def head_columns(zi, yy, of_core):
        return pl.ds(pl.multiple_of((yy * 4 + zi * 2 + of_core) * HD, HD), HD)

    mine_e, his_e = eraw.at[pl.ds(1 + 2 * core, 2)], eraw.at[pl.ds(1 + 2 * other, 2)]

    def whole_in(n, send_part):
        buf = (qraw, ctraw)[n]
        part = buf.at[rows if send_part else his_rows]
        return remote(part, part, in_send.at[n], in_recv.at[n], sibling)

    def exchange(n):
        src, dst = (q_hbm, qraw)[0:2] if n == 0 else (ct_hbm, ctraw)

        def body(j, carry):
            yy, zi = lax.div(j, 2), lax.rem(j, 2)
            to = dst.at[rows, pl.ds(pl.multiple_of(j * HD, HD), HD)]
            pltpu.make_async_copy(src.at[0, :, head_columns(zi, yy, core)], to, in_sem.at[n]).start()
            remote(src.at[0, :, head_columns(zi, yy, other)], to, in_send.at[n], in_recv.at[n], sibling).start()
            return carry

        lax.fori_loop(0, 16, body, 0)

    locals_ = {
        2: pltpu.make_async_copy(e_hbm.at[0], mine_e, in_sem.at[2]),
        3: pltpu.make_async_copy(ids_hbm.at[0], ids.at[1 + core], in_sem.at[3]),
    }
    sends = {
        2: remote(e_hbm.at[0], mine_e, in_send.at[2], in_recv.at[2], sibling),
        3: remote(ids_hbm.at[0], ids.at[1 + core], in_send.at[3], in_recv.at[3], sibling),
    }
    exchange(0)
    exchange(1)
    for n in (2, 3):
        locals_[n].start()
        sends[n].start()

    def in_wait(n):
        if n < 2:
            buf = (qraw, ctraw)[n]
            pltpu.make_async_copy(buf.at[rows], buf.at[rows], in_sem.at[n]).wait()
            whole_in(n, False).wait_recv()
        else:
            locals_[n].wait()
            to = his_e if n == 2 else ids.at[1 + other]
            remote(to, to, in_send.at[n], in_recv.at[n], sibling).wait_recv()

    def shift(n):
        raw, out = ((qraw, qs), (ctraw, cts))[n]
        in_wait(n)

        def body(j, carry):
            cols = pl.ds(pl.multiple_of(j * 256, 256), 256)
            moved = pltpu.roll(raw[:, cols].astype(jnp.float32), 1, 0).astype(jnp.bfloat16)
            out[0:256, cols] = moved
            out[256:272, cols] = moved[0:16]
            return carry

        lax.fori_loop(0, 8, body, 0)

    def pad(slots):
        def body(n, carry):
            block = eraw[n]
            at = pl.ds(pl.multiple_of(n * KEYS, KEYS), KEYS)
            e1[at, :] = dot(block, place1, TN).astype(jnp.bfloat16)
            e2[at, :] = dot(block, place2, TN).astype(jnp.bfloat16)
            return carry

        lax.fori_loop(slots[0], slots[1], body, 0)

    def prepare(n):
        if n < 2:
            shift(n)
        elif n == 2:
            in_wait(2)
            in_wait(3)
            pad((1, 3))
        elif n == 3:
            pad((3, 5))

    def zi_of(r):
        return zi_me if r == 0 else 1 - zi_me

    def row(i):
        return y + (4 if ROWS[i] == 4 else ROWS[i] * turn) + 8

    def along_x(r, i, side):
        here = piece(zi_of(r), row(i), x)
        at = side * 16 + r * 8 + i
        return remote(here, here, last_send.at[at], last_recv.at[at], peer("x", 1 if side == 0 else 3))

    def x_forward(r, i, side):
        there = piece(zi_of(r), row(i), x + (3 if side == 0 else 1))
        at = 32 + side * 16 + r * 8 + i
        half = there.at[pl.ds(16 * side, 16)]
        copy = remote(half, half, last_send.at[at], last_recv.at[at], peer("x", 1 if side == 0 else 3))
        return there, copy

    def x_pass_on(*numbers):
        for i, r in ((i, r) for i in numbers for r in range(2)):
            for side in range(2):
                there, copy = x_forward(r, i, side)
                at = side * 16 + r * 8 + i
                remote(there, there, last_send.at[0], last_recv.at[at], peer("x", 1)).wait_recv()
                copy.start()

    def x_passed(i):
        for r in range(2):
            there = piece(zi_of(r), row(i), x + 2)
            for side in range(2):
                half = there.at[pl.ds(16 * side, 16)]
                at = 32 + side * 16 + r * 8 + i
                remote(half, half, last_send.at[0], last_recv.at[at], peer("x", 1)).wait_recv()

    def y_side(i):
        return lax.div(1 + turn, 2) if ROWS[i] > 0 else lax.div(1 - turn, 2)

    def ring_copy(r, i, side, distance):
        here = piece(zi_of(r), row(i), x)
        if distance == 3:
            here = here.at[pl.ds(pl.multiple_of(16 * side, 16), 16)]
        at = side * 8 + distance * 2 + r
        t = 1 + 6 * side
        yy = lax.rem(y + t, 8)
        return remote(here, here, first_send.at[at], first_recv.at[at], (yy * 16 + zl * 4 + x, seq))

    def ring_wait(r, i, side, distance):
        there = piece(zi_of(r), row(i), x)
        if distance == 4:
            there = there.at[pl.ds(16 * side, 16)]
        at = side * 8 + (distance - 1) * 2 + r
        remote(there, there, first_send.at[0], first_recv.at[at], peer("y", 1)).wait_recv()

    def z_phase():
        @pl.when(is_source)
        def _():
            for t in (1, 3, 2):
                ensure("z", t)
                z_copy(0, t, mine).start()

        for r in range(2):
            if r == 0:
                pl.when(jnp.logical_not(is_source))(lambda: z_wait(zi_me, 0, mine))
            else:
                z_wait(1 - zi_me, 0, piece(1 - zi_me, y, x))
            for side in range(2):
                if r == 0:
                    ensure("y", 1 + 6 * side)
                    ensure("x", 1 + 2 * side)
                ring_copy(r, 0, side, 0).start()
                along_x(r, 0, side).start()

    def y_ring(distance):
        for i in range(1, 8):
            if abs(ROWS[i]) != distance:
                continue
            for r in range(2):
                if distance == 4:
                    ring_wait(r, i, 0, 4)
                    ring_wait(r, i, 1, 4)
                else:
                    ring_wait(r, i, y_side(i), distance)
                    ring_copy(r, i, y_side(i), distance).start()
                for side in range(2):
                    along_x(r, i, side).start()

    def along_y(r, j, side, distance):
        there = piece(zi_of(r), y + (8 - distance if side == 0 else distance) + 8, x + j)
        if distance == 3:
            there = there.at[pl.ds(16 * side, 16)]
        at = side * 32 + distance * 8 + r * 4 + j
        return remote(there, there, last_send.at[at], last_recv.at[at], peer("y", 1 if side == 0 else 7))

    def y_arrived(r, distance):
        for j in range(4):
            for side in range(2):
                there = piece(zi_of(r), y + (8 - distance if side == 0 else distance) + 8, x + j)
                if distance == 4:
                    there = there.at[pl.ds(16 * side, 16)]
                at = side * 32 + (distance - 1) * 8 + r * 4 + j
                remote(there, there, last_send.at[0], last_recv.at[at], peer("y", 1)).wait_recv()
                if distance < 4:
                    along_y(r, j, side, distance).start()

    def x_first(j):
        here = piece(zi_me, y, x + j)

        @pl.when(is_source)
        def _():
            if j:
                first_wait("x", j, here)
            for t in (1, 3, 2):
                if j == 0:
                    ensure("z", t)
                z_copy(j, t, here).start()

        @pl.when(jnp.logical_not(is_source))
        def _():
            z_wait(zi_me, j, here)

        for side in range(2):
            if j == 0:
                ensure("y", 1 if side == 0 else 7)
            along_y(0, j, side, 0).start()

    def x_second():
        for j in range(4):
            z_wait(1 - zi_me, j, piece(1 - zi_me, y, x + j))
            for side in range(2):
                along_y(1, j, side, 0).start()

    def prev_copies():
        return [
            remote(
                e_hbm.at[0, 1, pl.ds(224 * t, 224)], eraw.at[0, pl.ds(224 * t, 224)],
                prev_send.at[t], prev_recv.at[0], (dp, 2 + t),
            )
            for t in range(2)
        ] + [
            remote(ids_hbm.at[0], ids.at[0], prev_send.at[2 + t], prev_recv.at[1], (dp, 2 + t)) for t in range(2)
        ]

    @pl.when(core == 0)
    def _():
        z_phase()
        prepare(0)
        y_ring(1)
        prepare(1)
        x_pass_on(0)
        prepare(2)
        y_ring(2)
        prepare(3)
        x_pass_on(1, 2)

    @pl.when(core == 1)
    def _():
        for j in range(4):
            x_first(j)
            prepare(j)
        x_second()

        @pl.when(z_hi == 0)
        def _():
            for t in range(2):
                pl.semaphore_wait(ready.at[13 + t], 1)
            for copy in prev_copies():
                copy.start()

        y_arrived(0, 1)
        y_arrived(1, 1)

    def prev_on():
        half = eraw.at[0, pl.ds(pl.multiple_of(core * 224, 32), 224)]
        return remote(half, half, prev_send.at[4], prev_recv.at[2], sibling)

    def prev_arrived():
        half = eraw.at[0, pl.ds(pl.multiple_of(core * 224, 32), 224)]
        remote(half, half, prev_send.at[0], prev_recv.at[0], sibling).wait_recv()
        remote(ids.at[0], ids.at[0], prev_send.at[2], prev_recv.at[1], sibling).wait_recv()
        prev_on().start()

    def prev_whole():
        @pl.when(z_hi == 1)
        def _():
            half = eraw.at[0, pl.ds(pl.multiple_of(other * 224, 32), 224)]
            remote(half, half, prev_send.at[4], prev_recv.at[2], sibling).wait_recv()

        @pl.when(z_hi == 0)
        def _():
            eraw[0] = jnp.zeros((ENC, KEYS), jnp.bfloat16)
            ids[0] = jnp.zeros((2, KEYS), jnp.int32)

        pad((0, 1))

    def out_copies(step, head, col, out_col):
        found = []
        for n, (buf, out) in enumerate(((attbuf, att_hbm), (grbuf, gr_hbm))):
            at = (step * 2 + head) * 2 + n
            src = buf.at[his_rows, col]
            found.append(remote(src, out.at[:, out_col], out_send.at[at], out_recv.at[at], sibling))
            found.append(pltpu.make_async_copy(buf.at[rows, col], out.at[:, out_col], out_sem.at[at]))
        return found

    def columns(step, head, of_core):
        forth = jnp.where(jnp.logical_or(step == 0, step == 7), lax.div(step, 7) * 4, 0)
        for i in range(1, 7):
            forth = jnp.where(step == i, ROWS[i] * turn, forth)
        yy = lax.rem(y + forth + 8, 8)
        hh = yy * 2 + head
        return hh, pl.ds(pl.multiple_of(hh * HD, HD), HD), head_columns(head, yy, of_core)

    arrivals = (
        (
            lambda: None,
            lambda: (y_ring(3), x_pass_on(3, 4)),
            lambda: (y_ring(4), x_pass_on(5, 6)),
            lambda: x_pass_on(7),
        ),
        (
            lambda: None,
            lambda: y_arrived(0, 2),
            lambda: y_arrived(1, 2),
            lambda: y_arrived(0, 3),
            lambda: y_arrived(1, 3),
        ),
    )

    def work(step, carry):
        for c in range(2):
            for k, pass_on in enumerate(arrivals[c]):
                pl.when(jnp.logical_and(step == k, core == c))(lambda pass_on=pass_on: pass_on() and None)

        pl.when(jnp.logical_and(step == 0, z_hi == 1))(prev_arrived)
        turn_of = step - z_hi

        @pl.when(jnp.logical_and(turn_of >= 0, turn_of < 8))
        def _():
            attend(turn_of)

        return carry

    def attend(step):
        pl.when(step == 0)(prev_whole)
        for i in range(8):
            pl.when(jnp.logical_and(step == i, core == 0))(lambda i=i: x_passed(i))

        @pl.when(jnp.logical_and(step == 7, core == 1))
        def _():
            y_arrived(0, 4)
            y_arrived(1, 4)

        first = columns(step, 0, core)[0]
        cols = [columns(step, h, core)[1] for h in range(2)]
        wt = w[pl.ds(first, 2)].reshape(2 * HD, 2 * ENC)
        kb[...] = dot(e1[...], wt[:, 0:512], NT).astype(jnp.bfloat16)
        vb[...] = dot(e2[...], wt[:, 384:896], NT).astype(jnp.bfloat16)
        for h in range(2):
            hs = slice(h * HD, h * HD + HD)
            for g, (r, m) in enumerate(GROUP_ROWS):
                ks = slice(KEYS * g, KEYS * g + KEYS)
                sbuf[h, r:r + m] = dot(qs[r:r + m, cols[h]], kb[ks, hs], NT)
                dbuf[h, r:r + m] = dot(cts[r:r + m, cols[h]], vb[ks, hs], NT)
        for h in range(2):
            for g, (r, m) in enumerate(GROUP_ROWS):
                bias = jnp.where(ids[(g + 1) // 2, (g + 1) % 2:(g + 1) % 2 + 1, :] != 0, 0.0, MASKED)
                for c0 in range(r, r + m, CHUNK):
                    c1 = min(c0 + CHUNK, r + m)
                    pbuf[h, c0:c1], dsbuf[h, c0:c1] = softmax_parts(sbuf[h, c0:c1], dbuf[h, c0:c1], bias)
        for h in range(2):
            hs = slice(h * HD, h * HD + HD)
            for buf, weights, other_side in ((attbuf, pbuf, vb), (grbuf, dsbuf, kb)):
                parts = [
                    dot(weights[h, r:r + m], other_side[KEYS * g:KEYS * g + KEYS, hs], NN)
                    for g, (r, m) in enumerate(GROUP_ROWS)
                ]
                moved = pltpu.roll(jnp.concatenate(parts, 0), SHIFTED - 1, 0)
                buf[:, cols[h]] = moved[0:256].astype(jnp.bfloat16)
        for h in range(2):
            _, col, out_col = columns(step, h, core)
            for copy in out_copies(step, h, col, out_col):
                copy.start()

    lax.fori_loop(0, 9, work, 0)

    def finish(step, carry):
        for h in range(2):
            _, col, out_col = columns(step, h, core)
            _, _, his_col = columns(step, h, other)
            for n, copy in enumerate(out_copies(step, h, col, out_col)):
                if n % 2:
                    copy.wait()
                else:
                    copy.wait_send()
                    out = (att_hbm, gr_hbm)[n // 2]
                    at = (step * 2 + h) * 2 + n // 2
                    there = out.at[:, his_col]
                    remote(there, there, out_send.at[at], out_recv.at[at], sibling).wait_recv()
        return carry

    lax.fori_loop(0, 8, finish, 0)
    for n in range(2):
        whole_in(n, True).wait_send()
        sends[n + 2].wait_send()

    @pl.when(core == 0)
    def _():
        @pl.when(is_source)
        def _():
            for t in range(1, 4):
                z_copy(0, t, mine).wait_send()

        @pl.when(jnp.logical_not(is_source))
        def _():
            for t in range(1, 4):
                ensure("z", t)

        for r in range(2):
            for i in range(1, 7):
                ring_copy(r, i, y_side(i), abs(ROWS[i])).wait_send()
            for side in range(2):
                ring_copy(r, 0, side, 0).wait_send()

        for r in range(2):
            for i in range(8):
                for side in range(2):
                    along_x(r, i, side).wait_send()
                    x_forward(r, i, side)[1].wait_send()

    @pl.when(core == 1)
    def _():
        @pl.when(is_source)
        def _():
            for t in range(1, 4):
                first_copy("x", t).wait_send()
            for j in range(4):
                for t in range(1, 4):
                    z_copy(j, t, piece(zi_me, y, x + j)).wait_send()

        @pl.when(jnp.logical_not(is_source))
        def _():
            for t in range(1, 4):
                ensure("z", t)

        for r in range(2):
            for j in range(4):
                for side in range(2):
                    for distance in range(4):
                        along_y(r, j, side, distance).wait_send()

        @pl.when(z_hi == 0)
        def _():
            for copy in prev_copies():
                copy.wait_send()

    @pl.when(z_hi == 1)
    def _():
        prev_on().wait_send()


def on_device(queries, encodings, neighbour_ids, w_key, w_value, cotangent):
    bf16, f32, dma = jnp.bfloat16, jnp.float32, pltpu.SemaphoreType.DMA
    whole, anywhere = pl.BlockSpec(memory_space=pltpu.VMEM), pl.BlockSpec(memory_space=pl.ANY)
    attended, query_grad = pl.pallas_call(
        kernel,
        out_shape=(jax.ShapeDtypeStruct((128, WIDTH), bf16),) * 2,
        in_specs=[anywhere] * 4 + [whole] * 2,
        out_specs=(anywhere,) * 2,
        scratch_shapes=[
            pltpu.VMEM((16, 4, PIECE, 2 * ENC), bf16),
            pltpu.VMEM((256, HALF), bf16),
            pltpu.VMEM((256, HALF), bf16),
            pltpu.VMEM((SHIFTED, HALF), bf16),
            pltpu.VMEM((SHIFTED, HALF), bf16),
            pltpu.VMEM((GROUPS, ENC, KEYS), bf16),
            pltpu.VMEM((GROUPS * KEYS, 512), bf16),
            pltpu.VMEM((GROUPS * KEYS, 512), bf16),
            pltpu.VMEM((3, 2, KEYS), jnp.int32),
            pltpu.VMEM((GROUPS * KEYS, 2 * HD), bf16),
            pltpu.VMEM((GROUPS * KEYS, 2 * HD), bf16),
            pltpu.VMEM((2, SHIFTED, KEYS), f32),
            pltpu.VMEM((2, SHIFTED, KEYS), f32),
            pltpu.VMEM((2, SHIFTED, KEYS), bf16),
            pltpu.VMEM((2, SHIFTED, KEYS), bf16),
            pltpu.VMEM((256, HALF), bf16),
            pltpu.VMEM((256, HALF), bf16),
            pltpu.SemaphoreType.REGULAR((15,)),
            dma((4,)), dma((4,)), dma((4,)),
            dma((5,)), dma((3,)),
            dma((16,)), dma((16,)),
            dma((24,)), dma((16,)),
            dma((64,)), dma((64,)),
            dma((32,)), dma((32,)), dma((32,)),
        ],
        compiler_params=pltpu.CompilerParams(
            collective_id=0, has_side_effects=True, vmem_limit_bytes=60 << 20
        ),
    )(queries, cotangent, jnp.swapaxes(encodings, 2, 3), neighbour_ids, w_key.T, w_value.T)
    return attended[None], query_grad[None]


def solution(mesh):
    return jax.shard_map(
        on_device,
        mesh=mesh,
        in_specs=(
            P("dp", "seq", None),
            P("dp", "seq", None, None),
            P("dp", "seq", None),
            P(None, "dp"),
            P(None, "dp"),
            P("dp", "seq", None),
        ),
        out_specs=(P("dp", "seq", None), P("dp", "seq", None)),
        check_vma=False,
    )
```

time: 62.5 us -> 54.7 us (0.88)
  Pallas kernels: 56.1 us -> 50.5 us
  local copies, waits for them, and re-layouts: 5.53 us -> 3.35 us
    pallas_call x1, Pallas kernels: 56.1 us -> 50.5 us  [on_device(): pl.pallas_call(kernel, out_shape=(jax.ShapeDtypeStruct((128, WIDTH), bf16...]
    unnamed x13 -> x4, local copies, waits for them, and re-layouts: 5.53 us -> 3.35 us
where the time goes in v2:
time: 54.7 us; the launch traced here: 54.5 us
  Pallas kernels  50.5 us (92%)
  local copies, waits for them, and re-layouts  3.35 us (6%)
  between operations  0.65 us (1%)
    pallas_call x1, Pallas kernels, on_device(): pl.pallas_call(kernel, out_shape=(jax.ShapeDtypeStruct((128, WIDTH), bf16...  50.5 us
    unnamed x4, local copies, waits for them, and re-layouts  3.35 us

profile of v2, /device:TPU:1, one launch (start us, length us, event | category | flops | bytes accessed | tf_op | source)
XLA Modules:
  0.0 54.5 jit_solution(15959163614684571393)
XLA Ops:
  0.6 50.5 %shard_map.77 = (bf16[128,4096]{1,0:T(8,128)(2,1)}, bf16[128,4096]{1,0:T(8,128)(2,1)}) custom-call(bf16[1,128,4096]{2,1,0:T(8,128)(2,1)} %q_hbm.1, bf16[1,128,4096]{2,1,0:T(8,128)(2,1)} %ct_hbm.1, bf16[1,2,448,256]{3,2,1,0:T(8,128)(2,1)} %bitcast.7, s32[1,2,256]{2,1,0:T(2,128)} %ids_hbm.1, bf16[32,448]{1,0:T(8,128)(2,1)} %bitcast.8, bf16[32,448]{1,0:T(8,128)(2,1)} %bitcast.9), custom_call_target="tpu_custom_call" | custom-call | tf_op jit(solution)/shard_map/pallas_call | solution.py:618
  51.1 0.0 copy-start
  51.1 2.4 %copy.10 = bf16[1,128,4096]{2,1,0:T(8,128)(2,1)} copy(bf16[1,128,4096]{2,1,0:T(8,128)(2,1)} %bitcast.6) | data formatting | bytes 2097152
  53.5 0.0 copy-done
  53.5 1.0 %copy.11 = bf16[1,128,4096]{2,1,0:T(8,128)(2,1)} copy(bf16[1,128,4096]{2,1,0:T(8,128)(2,1)S(1)} %bitcast.5) | data formatting | bytes 2097152
Async XLA Ops:
  51.1 2.4 %copy-start = (bf16[128,4096]{1,0:T(8,128)(2,1)S(1)}, bf16[128,4096]{1,0:T(8,128)(2,1)}, u32[]{:S(2)}) copy-start(bf16[128,4096]{1,0:T(8,128)(2,1)} %get-tuple-element.5) | copy-start | bytes 3145732

commit v3 on v2

--- a/solution.py
+++ b/solution.py
@@ -82,17 +82,11 @@
 
     sizes = {"y": 8, "x": 4, "z": 4}
     sibling = (dp, z_hi * 2 + other)
-    source1 = jnp.logical_and(is_source, core == 1)
-
-    edges = [("z", t, True) for t in range(1, 4)] + [("x", t, core == 0) for t in (1, 3)]
+
+    edges = [("z", t, True) for t in range(1, 4)] + [("x", t, True) for t in (1, 3)] + [("x", 2, core == 1)]
     edges += [("y", t, True) for t in (1, 7)]
     gives_prev = jnp.logical_and(z_hi == 0, core == 1)
-    count = 1 + jnp.where(z_hi == 1, 1, 0) + jnp.where(source1, 3, 0)
-
-    @pl.when(source1)
-    def _():
-        for t in (2, 1, 3):
-            pl.semaphore_signal(barrier, inc=1, device_id=peer("x", t), device_id_type=MESH)
+    count = 1 + jnp.where(z_hi == 1, 1, 0)
 
     for axis, t, active in edges:
         after = jnp.logical_and(active, later(axis, t))
@@ -133,16 +127,7 @@
             src_ref=src, dst_ref=dst, send_sem=send, recv_sem=recv, device_id=to, device_id_type=MESH
         )
 
-    def first_copy(axis, t):
-        back = sizes[axis] - t
-        return remote(mine, mine, first_send.at[t - 1], first_recv.at[back - 1], peer(axis, t))
-
     pl.semaphore_wait(barrier, count)
-
-    @pl.when(source1)
-    def _():
-        for t in (2, 1, 3):
-            first_copy("x", t).start()
 
     for axis, t, active in edges:
         before = jnp.logical_and(active, jnp.logical_not(later(axis, t)))
@@ -161,9 +146,6 @@
         @pl.when(later(axis, t))
         def _():
             pl.semaphore_wait(ready.at[slot(axis, t)], 1)
-
-    def first_wait(axis, t, there):
-        remote(there, there, first_send.at[0], first_recv.at[t - 1], peer(axis, 1)).wait_recv()
 
     def z_copy(i, t, here):
         return remote(here, here, z_send.at[i * 3 + t - 1], z_recv.at[zi_me * 8 + i], peer("z", t))
@@ -306,24 +288,33 @@
         at = side * 8 + (distance - 1) * 2 + r
         remote(there, there, first_send.at[0], first_recv.at[at], peer("y", 1)).wait_recv()
 
-    def z_phase():
-        @pl.when(is_source)
-        def _():
-            for t in (1, 3, 2):
-                ensure("z", t)
+    def z_phase(forward):
+        def to_later(t):
+            @pl.when(jnp.logical_and(is_source, later("z", t)))
+            def _():
+                pl.semaphore_wait(ready.at[slot("z", t)], 1)
                 z_copy(0, t, mine).start()
 
-        for r in range(2):
+        for t in (1, 2, 3):
+            @pl.when(jnp.logical_and(is_source, jnp.logical_not(later("z", t))))
+            def _():
+                z_copy(0, t, mine).start()
+
+        to_later(1)
+        to_later(2)
+        pl.when(jnp.logical_not(is_source))(lambda: z_wait(zi_me, 0, mine))
+        forward(0)
+        to_later(3)
+        z_wait(1 - zi_me, 0, piece(1 - zi_me, y, x))
+        forward(1)
+
+    def z_forward(r):
+        for side in range(2):
             if r == 0:
-                pl.when(jnp.logical_not(is_source))(lambda: z_wait(zi_me, 0, mine))
-            else:
-                z_wait(1 - zi_me, 0, piece(1 - zi_me, y, x))
-            for side in range(2):
-                if r == 0:
-                    ensure("y", 1 + 6 * side)
-                    ensure("x", 1 + 2 * side)
-                ring_copy(r, 0, side, 0).start()
-                along_x(r, 0, side).start()
+                ensure("y", 1 + 6 * side)
+                ensure("x", 1 + 2 * side)
+            ring_copy(r, 0, side, 0).start()
+            along_x(r, 0, side).start()
 
     def y_ring(distance):
         for i in range(1, 8):
@@ -357,32 +348,26 @@
                 if distance < 4:
                     along_y(r, j, side, distance).start()
 
-    def x_first(j):
-        here = piece(zi_me, y, x + j)
-
-        @pl.when(is_source)
-        def _():
-            if j:
-                first_wait("x", j, here)
-            for t in (1, 3, 2):
-                if j == 0:
-                    ensure("z", t)
-                z_copy(j, t, here).start()
-
-        @pl.when(jnp.logical_not(is_source))
-        def _():
-            z_wait(zi_me, j, here)
-
+    def x_copy(r, t):
+        here = piece(zi_of(r), y, x)
+        return remote(here, here, first_send.at[r * 3 + t - 1], first_recv.at[r * 3 + 3 - t], peer("x", t))
+
+    def x_forward_first(r):
+        for t in (2, 1, 3):
+            if r == 0:
+                ensure("x", t)
+            x_copy(r, t).start()
         for side in range(2):
-            if j == 0:
-                ensure("y", 1 if side == 0 else 7)
-            along_y(0, j, side, 0).start()
-
-    def x_second():
-        for j in range(4):
-            z_wait(1 - zi_me, j, piece(1 - zi_me, y, x + j))
+            if r == 0:
+                ensure("y", 1 + 6 * side)
+            along_y(r, 0, side, 0).start()
+
+    def x_phase(r):
+        for j in (1, 3, 2):
+            there = piece(zi_of(r), y, x + j)
+            remote(there, there, first_send.at[0], first_recv.at[r * 3 + j - 1], peer("x", 1)).wait_recv()
             for side in range(2):
-                along_y(1, j, side, 0).start()
+                along_y(r, j, side, 0).start()
 
     def prev_copies():
         return [
@@ -397,7 +382,7 @@
 
     @pl.when(core == 0)
     def _():
-        z_phase()
+        z_phase(z_forward)
         prepare(0)
         y_ring(1)
         prepare(1)
@@ -409,10 +394,12 @@
 
     @pl.when(core == 1)
     def _():
-        for j in range(4):
-            x_first(j)
-            prepare(j)
-        x_second()
+        z_phase(x_forward_first)
+        prepare(0)
+        x_phase(0)
+        x_phase(1)
+        for n in range(1, 4):
+            prepare(n)
 
         @pl.when(z_hi == 0)
         def _():
@@ -447,13 +434,12 @@
 
         pad((0, 1))
 
-    def out_copies(step, head, col, out_col):
+    def out_copies(col, out_col):
         found = []
         for n, (buf, out) in enumerate(((attbuf, att_hbm), (grbuf, gr_hbm))):
-            at = (step * 2 + head) * 2 + n
             src = buf.at[his_rows, col]
-            found.append(remote(src, out.at[:, out_col], out_send.at[at], out_recv.at[at], sibling))
-            found.append(pltpu.make_async_copy(buf.at[rows, col], out.at[:, out_col], out_sem.at[at]))
+            found.append(remote(src, out.at[:, out_col], out_send.at[n], out_recv.at[n], sibling))
+            found.append(pltpu.make_async_copy(buf.at[rows, col], out.at[:, out_col], out_sem.at[n]))
         return found
 
     def columns(step, head, of_core):
@@ -532,27 +518,16 @@
                 buf[:, cols[h]] = moved[0:256].astype(jnp.bfloat16)
         for h in range(2):
             _, col, out_col = columns(step, h, core)
-            for copy in out_copies(step, h, col, out_col):
+            for copy in out_copies(col, out_col):
                 copy.start()
 
     lax.fori_loop(0, 9, work, 0)
 
-    def finish(step, carry):
-        for h in range(2):
-            _, col, out_col = columns(step, h, core)
-            _, _, his_col = columns(step, h, other)
-            for n, copy in enumerate(out_copies(step, h, col, out_col)):
-                if n % 2:
-                    copy.wait()
-                else:
-                    copy.wait_send()
-                    out = (att_hbm, gr_hbm)[n // 2]
-                    at = (step * 2 + h) * 2 + n // 2
-                    there = out.at[:, his_col]
-                    remote(there, there, out_send.at[at], out_recv.at[at], sibling).wait_recv()
-        return carry
-
-    lax.fori_loop(0, 8, finish, 0)
+    for n, buf in enumerate((attbuf, grbuf)):
+        pltpu.make_async_copy(buf.at[rows], buf.at[rows], out_sem.at[n]).wait()
+        whole = remote(buf.at[rows], buf.at[rows], out_send.at[n], out_recv.at[n], sibling)
+        whole.wait_send()
+        whole.wait_recv()
     for n in range(2):
         whole_in(n, True).wait_send()
         sends[n + 2].wait_send()
@@ -586,16 +561,16 @@
         @pl.when(is_source)
         def _():
             for t in range(1, 4):
-                first_copy("x", t).wait_send()
-            for j in range(4):
-                for t in range(1, 4):
-                    z_copy(j, t, piece(zi_me, y, x + j)).wait_send()
+                z_copy(0, t, mine).wait_send()
 
         @pl.when(jnp.logical_not(is_source))
         def _():
             for t in range(1, 4):
                 ensure("z", t)
 
+        for r in range(2):
+            for t in range(1, 4):
+                x_copy(r, t).wait_send()
         for r in range(2):
             for j in range(4):
                 for side in range(2):
@@ -610,6 +585,20 @@
     @pl.when(z_hi == 1)
     def _():
         prev_on().wait_send()
+
+
+def hand_over(att_in, gr_in, att_out, gr_out, att_buf, gr_buf, in_sem, out_sem):
+    arrays = ((att_in, att_buf, att_out), (gr_in, gr_buf, gr_out))
+    parts = [(n, i, pl.ds(32 * i, 32)) for i in range(4) for n in range(2)]
+    loads = [pltpu.make_async_copy(arrays[n][0].at[at], arrays[n][1].at[at], in_sem.at[n, i]) for n, i, at in parts]
+    stores = [pltpu.make_async_copy(arrays[n][1].at[at], arrays[n][2].at[at], out_sem.at[n, i]) for n, i, at in parts]
+    for load in loads:
+        load.start()
+    for load, store in zip(loads, stores):
+        load.wait()
+        store.start()
+    for store in stores:
+        store.wait()
 
 
 def on_device(queries, encodings, neighbour_ids, w_key, w_value, cotangent):
@@ -644,12 +633,19 @@
             dma((16,)), dma((16,)),
             dma((24,)), dma((16,)),
             dma((64,)), dma((64,)),
-            dma((32,)), dma((32,)), dma((32,)),
+            dma((2,)), dma((2,)), dma((2,)),
         ],
         compiler_params=pltpu.CompilerParams(
             collective_id=0, has_side_effects=True, vmem_limit_bytes=60 << 20
         ),
     )(queries, cotangent, jnp.swapaxes(encodings, 2, 3), neighbour_ids, w_key.T, w_value.T)
+    attended, query_grad = pl.pallas_call(
+        hand_over,
+        out_shape=(jax.ShapeDtypeStruct((128, WIDTH), bf16),) * 2,
+        in_specs=[anywhere] * 2,
+        out_specs=(anywhere,) * 2,
+        scratch_shapes=[pltpu.VMEM((128, WIDTH), bf16)] * 2 + [dma((2, 4)), dma((2, 4))],
+    )(attended, query_grad)
     return attended[None], query_grad[None]
 
 

time: 54.7 us -> 49.6 us (0.907)
  local copies, waits for them, and re-layouts: 3.35 us -> 0 us
  Pallas kernels: 50.5 us -> 48.5 us
    pallas_call x1, Pallas kernels: 50.5 us -> 46.1 us  [on_device(): pl.pallas_call(kernel, out_shape=(jax.ShapeDtypeStruct((128, WIDTH), bf16...]
    unnamed x4 -> x0, local copies, waits for them, and re-layouts: 3.35 us -> none
    pallas_call x0 -> x1, Pallas kernels: none -> 2.39 us  [on_device(): pl.pallas_call(hand_over, out_shape=(jax.ShapeDtypeStruct((128, WIDTH), b...]
where the time goes in v3:
time: 49.6 us; the launch traced here: 49.1 us
  Pallas kernels  48.5 us (98%)
  between operations  0.64 us (1%)
    pallas_call x1, Pallas kernels, on_device(): pl.pallas_call(kernel, out_shape=(jax.ShapeDtypeStruct((128, WIDTH), bf16...  46.1 us
    pallas_call x1, Pallas kernels, on_device(): pl.pallas_call(hand_over, out_shape=(jax.ShapeDtypeStruct((128, WIDTH), b...  2.39 us

profile of v3, /device:TPU:1, one launch (start us, length us, event | category | flops | bytes accessed | tf_op | source)
XLA Modules:
  0.0 49.1 jit_solution(8021306543096186549)
XLA Ops:
  0.6 46.1 %shard_map.77 = (bf16[128,4096]{1,0:T(8,128)(2,1)}, bf16[128,4096]{1,0:T(8,128)(2,1)}) custom-call(bf16[1,128,4096]{2,1,0:T(8,128)(2,1)} %q_hbm.1, bf16[1,128,4096]{2,1,0:T(8,128)(2,1)} %ct_hbm.1, bf16[1,2,448,256]{3,2,1,0:T(8,128)(2,1)} %bitcast.5, s32[1,2,256]{2,1,0:T(2,128)} %ids_hbm.1, bf16[32,448]{1,0:T(8,128)(2,1)} %bitcast.6, bf16[32,448]{1,0:T(8,128)(2,1)} %bitcast.7), custom_call_target="tpu_custom_call" | custom-call | tf_op jit(solution)/shard_map/pallas_call | solution.py:607
  46.7 2.4 %shard_map.78 = (bf16[128,4096]{1,0:T(8,128)(2,1)}, bf16[128,4096]{1,0:T(8,128)(2,1)}) custom-call(bf16[128,4096]{1,0:T(8,128)(2,1)} %get-tuple-element.6.att_in, bf16[128,4096]{1,0:T(8,128)(2,1)} %get-tuple-element.7.gr_in), custom_call_target="tpu_custom_call" | custom-call | tf_op jit(solution)/shard_map/pallas_call | solution.py:642

commit v4 on v3

--- a/solution.py
+++ b/solution.py
@@ -244,13 +244,12 @@
     def along_x(r, i, side):
         here = piece(zi_of(r), row(i), x)
         at = side * 16 + r * 8 + i
-        return remote(here, here, last_send.at[at], last_recv.at[at], peer("x", 1 if side == 0 else 3))
+        return remote(here, here, last_send.at[0], last_recv.at[at], peer("x", 1 if side == 0 else 3))
 
     def x_forward(r, i, side):
         there = piece(zi_of(r), row(i), x + (3 if side == 0 else 1))
-        at = 32 + side * 16 + r * 8 + i
         half = there.at[pl.ds(16 * side, 16)]
-        copy = remote(half, half, last_send.at[at], last_recv.at[at], peer("x", 1 if side == 0 else 3))
+        copy = remote(half, half, last_send.at[0], last_recv.at[32 + i], peer("x", 1 if side == 0 else 3))
         return there, copy
 
     def x_pass_on(*numbers):
@@ -262,12 +261,8 @@
                 copy.start()
 
     def x_passed(i):
-        for r in range(2):
-            there = piece(zi_of(r), row(i), x + 2)
-            for side in range(2):
-                half = there.at[pl.ds(16 * side, 16)]
-                at = 32 + side * 16 + r * 8 + i
-                remote(half, half, last_send.at[0], last_recv.at[at], peer("x", 1)).wait_recv()
+        there = w.at[pl.ds(lax.rem(row(i), 8) * 2, 2), lax.rem(x + 2, 4)]
+        remote(there, there, last_send.at[0], last_recv.at[32 + i], peer("x", 1)).wait_recv()
 
     def y_side(i):
         return lax.div(1 + turn, 2) if ROWS[i] > 0 else lax.div(1 - turn, 2)
@@ -334,19 +329,20 @@
         there = piece(zi_of(r), y + (8 - distance if side == 0 else distance) + 8, x + j)
         if distance == 3:
             there = there.at[pl.ds(16 * side, 16)]
-        at = side * 32 + distance * 8 + r * 4 + j
-        return remote(there, there, last_send.at[at], last_recv.at[at], peer("y", 1 if side == 0 else 7))
+        at = 24 if distance == 3 else side * 32 + distance * 8 + r * 4 + j
+        return remote(there, there, last_send.at[0], last_recv.at[at], peer("y", 1 if side == 0 else 7))
 
     def y_arrived(r, distance):
         for j in range(4):
             for side in range(2):
                 there = piece(zi_of(r), y + (8 - distance if side == 0 else distance) + 8, x + j)
-                if distance == 4:
-                    there = there.at[pl.ds(16 * side, 16)]
                 at = side * 32 + (distance - 1) * 8 + r * 4 + j
                 remote(there, there, last_send.at[0], last_recv.at[at], peer("y", 1)).wait_recv()
-                if distance < 4:
-                    along_y(r, j, side, distance).start()
+                along_y(r, j, side, distance).start()
+
+    def y_far():
+        there = w.at[pl.ds(lax.rem(y + 4, 8) * 2, 2)]
+        remote(there, there, last_send.at[0], last_recv.at[24], peer("y", 1)).wait_recv()
 
     def x_copy(r, t):
         here = piece(zi_of(r), y, x)
@@ -487,8 +483,7 @@
 
         @pl.when(jnp.logical_and(step == 7, core == 1))
         def _():
-            y_arrived(0, 4)
-            y_arrived(1, 4)
+            y_far()
 
         first = columns(step, 0, core)[0]
         cols = [columns(step, h, core)[1] for h in range(2)]
@@ -550,11 +545,8 @@
             for side in range(2):
                 ring_copy(r, 0, side, 0).wait_send()
 
-        for r in range(2):
-            for i in range(8):
-                for side in range(2):
-                    along_x(r, i, side).wait_send()
-                    x_forward(r, i, side)[1].wait_send()
+        sent = w.at[pl.ds(0, 12)]
+        remote(sent, sent, last_send.at[0], last_recv.at[0], peer("x", 1)).wait_send()
 
     @pl.when(core == 1)
     def _():
@@ -571,11 +563,8 @@
         for r in range(2):
             for t in range(1, 4):
                 x_copy(r, t).wait_send()
-        for r in range(2):
-            for j in range(4):
-                for side in range(2):
-                    for distance in range(4):
-                        along_y(r, j, side, distance).wait_send()
+        sent = w.at[pl.ds(0, 14)]
+        remote(sent, sent, last_send.at[0], last_recv.at[0], peer("y", 1)).wait_send()
 
         @pl.when(z_hi == 0)
         def _():
@@ -632,7 +621,7 @@
             dma((5,)), dma((3,)),
             dma((16,)), dma((16,)),
             dma((24,)), dma((16,)),
-            dma((64,)), dma((64,)),
+            dma((1,)), dma((64,)),
             dma((2,)), dma((2,)), dma((2,)),
         ],
         compiler_params=pltpu.CompilerParams(

time: 49.6 us -> 48.8 us (0.984)
  Pallas kernels: 48.5 us -> 47.7 us
    pallas_call x1, Pallas kernels: 46.1 us -> 45.3 us  [on_device(): pl.pallas_call(kernel, out_shape=(jax.ShapeDtypeStruct((128, WIDTH), bf16...]
where the time goes in v4:
time: 48.8 us; the launch traced here: 48.3 us
  Pallas kernels  47.7 us (98%)
  between operations  0.64 us (1%)
    pallas_call x1, Pallas kernels, on_device(): pl.pallas_call(kernel, out_shape=(jax.ShapeDtypeStruct((128, WIDTH), bf16...  45.3 us
    pallas_call x1, Pallas kernels, on_device(): pl.pallas_call(hand_over, out_shape=(jax.ShapeDtypeStruct((128, WIDTH), b...  2.39 us

profile of v4, /device:TPU:1, one launch (start us, length us, event | category | flops | bytes accessed | tf_op | source)
XLA Modules:
  0.0 48.3 jit_solution(4569081893040489284)
XLA Ops:
  0.6 45.3 %shard_map.77 = (bf16[128,4096]{1,0:T(8,128)(2,1)}, bf16[128,4096]{1,0:T(8,128)(2,1)}) custom-call(bf16[1,128,4096]{2,1,0:T(8,128)(2,1)} %q_hbm.1, bf16[1,128,4096]{2,1,0:T(8,128)(2,1)} %ct_hbm.1, bf16[1,2,448,256]{3,2,1,0:T(8,128)(2,1)} %bitcast.5, s32[1,2,256]{2,1,0:T(2,128)} %ids_hbm.1, bf16[32,448]{1,0:T(8,128)(2,1)} %bitcast.6, bf16[32,448]{1,0:T(8,128)(2,1)} %bitcast.7), custom_call_target="tpu_custom_call" | custom-call | tf_op jit(solution)/shard_map/pallas_call | solution.py:596
  45.9 2.4 %shard_map.78 = (bf16[128,4096]{1,0:T(8,128)(2,1)}, bf16[128,4096]{1,0:T(8,128)(2,1)}) custom-call(bf16[128,4096]{1,0:T(8,128)(2,1)} %get-tuple-element.6.att_in, bf16[128,4096]{1,0:T(8,128)(2,1)} %get-tuple-element.7.gr_in), custom_call_target="tpu_custom_call" | custom-call | tf_op jit(solution)/shard_map/pallas_call | solution.py:631
